TPU v7x, 768 devices: a whole 4x8x12 slice. The times are simulated.
768 devices in a mesh: nodes: 64 (over y, x, core), feat: 12 (over z).
Axes of the slice: x: 4, y: 8, z: 12, core: 2. Of those that a mesh axis runs over, the one named last changes fastest.
Arguments:
- features: bfloat16 [65536, 1152], P('nodes', 'feat'), may hold values from -6 to 6
- w_neigh: bfloat16 [1152, 256], P('feat'), may hold values from -0.1875 to 0.1875
- w_self: bfloat16 [1152, 256], P('feat'), may hold values from -0.1875 to 0.1875
- bias: float32 [256], replicated, may hold values from -3 to 3
- target_blocks: int32 [384], P('nodes'), may hold values from 0 to 7, as said below
- loc_tiles: bfloat16 [384, 8, 128, 128], P('nodes'), may hold values from -0.25 to 0.25
- loc_src: int32 [384, 8], P('nodes'), may hold values from 0 to 7
- loc_count: int32 [384], P('nodes'), may hold values from 1 to 8, as said below
- rem_tiles: bfloat16 [64, 64, 128, 128], P('nodes'), may hold values from -0.25 to 0.25
- rem_src: int32 [64, 64], P('nodes'), may hold values from 0 to 7
- rem_slot: int32 [64, 64], P('nodes'), may hold values from 0 to 5
- degree: int32 [49152], P('nodes'), may hold values from 1 to 8
- cotangent: bfloat16 [49152, 256], P(('nodes', 'feat')), may hold values from -6 to 6
Outputs:
- activation: bfloat16 [49152, 256], P(('nodes', 'feat'))
- grad_neigh: float32 [1152, 256], P('feat')
- grad_self: float32 [1152, 256], P('feat')
- grad_bias: float32 [256], replicated
Inputs may be any that keep to these rules, and one draw needn't show every extreme that they name: `target_blocks`: the 6 ids of one index of nodes are distinct local block ids. Tiles k < loc_count[t] of target block t are in use, the others are ignored.
All inputs are finite; a program needn't handle non-finite values.
Results may differ from a plain program's by a relative error of at most 0.007.
Values may be sent and summed in bfloat16 or wider, within the bound.
A program may use at most 32 MiB of HBM per device.

v0:
```python
import jax
import jax.numpy as jnp
from jax import lax
from jax.sharding import PartitionSpec as P


def gelu_slope(pre_act, upstream):
    _, pullback = jax.vjp(lambda value: jax.nn.gelu(value, approximate=True), pre_act)
    return pullback(upstream)[0]


def local(
    features,
    w_neigh,
    w_self,
    bias,
    target_blocks,
    loc_tiles,
    loc_src,
    loc_count,
    rem_tiles,
    rem_src,
    rem_slot,
    degree,
    cotangent,
):
    block_size = loc_tiles.shape[-1]
    col_width = features.shape[1]
    own_blocks = features.shape[0] // block_size
    target_count = target_blocks.shape[0]
    slot_total = loc_tiles.shape[1]
    peer_count = lax.axis_size("nodes")
    row_count = target_count * block_size
    blocks = features.reshape(own_blocks, block_size, col_width)
    chosen = blocks[rem_src[0]]
    outgoing = jnp.einsum(
        "dij,djf->dif", rem_tiles[0], chosen, preferred_element_type=jnp.float32
    ).astype(jnp.bfloat16)
    incoming = lax.all_to_all(outgoing, "nodes", split_axis=0, concat_axis=0, tiled=True)
    in_use = jnp.arange(slot_total, dtype=jnp.int32)[None, :] < loc_count[:, None]
    masked = jnp.where(in_use[:, :, None, None], loc_tiles, jnp.zeros((), jnp.bfloat16))
    gathered = blocks[loc_src]
    nearby = jnp.einsum("tkij,tkjf->tif", masked, gathered, preferred_element_type=jnp.float32)
    landing = (rem_slot[0][None, :] == jnp.arange(target_count, dtype=jnp.int32)[:, None]).astype(
        jnp.bfloat16
    )
    remote = jnp.dot(
        landing,
        incoming.reshape(peer_count, block_size * col_width),
        preferred_element_type=jnp.float32,
    )
    summed = (nearby + remote.reshape(target_count, block_size, col_width)).reshape(
        row_count, col_width
    )
    aggregated = (summed / degree.astype(jnp.float32)[:, None]).astype(jnp.bfloat16)
    own_rows = blocks[target_blocks].reshape(row_count, col_width)
    agg_owned, rows_owned = (
        lax.all_to_all(aggregated, "feat", split_axis=0, concat_axis=1, tiled=True),
        lax.all_to_all(own_rows, "feat", split_axis=0, concat_axis=1, tiled=True),
    )
    neigh_full, self_full = (
        lax.all_gather(w_neigh, "feat", axis=0, tiled=True),
        lax.all_gather(w_self, "feat", axis=0, tiled=True),
    )
    pre_act = (
        jnp.dot(agg_owned, neigh_full, preferred_element_type=jnp.float32)
        + jnp.dot(rows_owned, self_full, preferred_element_type=jnp.float32)
        + bias
    )
    activation = jax.nn.gelu(pre_act, approximate=True).astype(jnp.bfloat16)
    slopes = gelu_slope(pre_act, cotangent.astype(jnp.float32)).astype(jnp.bfloat16)
    neigh_terms = jnp.dot(agg_owned.T, slopes, preferred_element_type=jnp.float32)
    self_terms = jnp.dot(rows_owned.T, slopes, preferred_element_type=jnp.float32)
    grad_neigh, grad_self = (
        lax.psum_scatter(neigh_terms, "feat", scatter_dimension=0, tiled=True),
        lax.psum_scatter(self_terms, "feat", scatter_dimension=0, tiled=True),
    )
    grad_neigh, grad_self = lax.psum((grad_neigh, grad_self), "nodes")
    grad_bias = lax.psum(jnp.sum(slopes.astype(jnp.float32), axis=0), ("nodes", "feat"))
    return (activation, grad_neigh, grad_self, grad_bias)


def solution(mesh):
    return jax.shard_map(
        local,
        mesh=mesh,
        in_specs=(
            P("nodes", "feat"),
            P("feat", None),
            P("feat", None),
            P(),
            P("nodes"),
            P("nodes", None, None, None),
            P("nodes", None),
            P("nodes"),
            P("nodes", None, None, None),
            P("nodes", None),
            P("nodes", None),
            P("nodes"),
            P(("nodes", "feat"), None),
        ),
        out_specs=(P(("nodes", "feat"), None), P("feat", None), P("feat", None), P()),
        check_vma=False,
    )
```

profile of v0, /device:TPU:1, one launch (start us, length us, event | category | flops | bytes accessed | tf_op | source)
XLA Modules:
  0.0 496.6 jit_solution(17568803886645766948)
XLA Ops:
  7.2 0.0 copy-start
  7.2 1.1 copy_bitcast_fusion
  8.3 0.7 fusion.33
  9.0 1.9 gather_fusion.1
  10.9 4.1 fusion.8
  15.0 15.5 %all-to-all-start = ((bf16[64,128,96]{1,2,0:T(8,128)(2,1)}), bf16[64,128,96]{1,2,0:T(8,128)(2,1)}, u32[]{:S(2)}, u32[]{:S(2)}) async-start(bf16[64,128,96]{1,2,0:T(8,128)(2,1)} %fusion.8), calls=%async_computation | async-start | bytes 3145728 | tf_op jit(solution)/shard_map/all_to_all | solution.py:39
  30.6 0.1 reshape.89
  30.7 0.0 copy-start.9
  30.7 0.8 gather_fusion
  31.5 0.1 div.11
  31.6 1.2 gather_fusion.2
  32.8 1.7 copy.34
  34.5 0.1 iota_compare_fusion.1
  34.6 35.0 %all-to-all-done = bf16[64,128,96]{1,2,0:T(8,128)(2,1)} async-done(((bf16[64,128,96]{1,2,0:T(8,128)(2,1)}), bf16[64,128,96]{1,2,0:T(8,128)(2,1)}, u32[]{:S(2)}, u32[]{:S(2)}) %all-to-all-start) | async-done | bytes 1572896 | tf_op jit(solution)/shard_map/all_to_all | solution.py:39
  69.6 11.2 %all-to-all-start.2 = ((bf16[12,64,96]{2,1,0:T(8,128)(2,1)}), bf16[12,64,96]{2,1,0:T(8,128)(2,1)}, u32[]{:S(2)}, u32[]{:S(2)}) async-start(bf16[12,64,96]{2,1,0:T(8,128)(2,1)} %bitcast.12), calls=%async_computation.2 | async-start | bytes 393216 | tf_op jit(solution)/shard_map/all_to_all | solution.py:59
  80.8 3.8 copy.28
  84.6 5.0 %reshape.85 = bf16[64,12288]{1,0:T(8,128)(2,1)} reshape(bf16[64,128,96]{2,1,0:T(8,128)(2,1)} %copy.28) | data formatting | bytes 3145728 | tf_op jit(solution)/shard_map/reshape | solution.py:49
  89.6 4.5 dot_general.28
  94.1 3.9 copy.29
  98.0 1.8 fusion.30
  99.8 0.0 copy-done.6
  99.8 1.4 fusion.14
  101.3 1.1 copy.31
  102.4 0.9 divide_convert_fusion
  103.3 9.0 %all-to-all-start.1 = ((bf16[12,64,96]{2,1,0:T(8,128)(2,1)}), bf16[12,64,96]{2,1,0:T(8,128)(2,1)S(1)}, u32[]{:S(2)}, u32[]{:S(2)}) async-start(bf16[12,64,96]{2,1,0:T(8,128)(2,1)} %divide_convert_fusion), calls=%async_computation.1 | async-start | bytes 393216 | tf_op jit(solution)/shard_map/all_to_all | solution.py:58
  112.3 0.0 reduce-scatter.3.cloned.1.call-start
  112.4 24.1 %all_gather.6 = bf16[1152,256]{1,0:T(8,128)(2,1)S(1)} all-gather(bf16[96,256]{1,0:T(8,128)(2,1)S(1)} %copy-done.1), channel_id=1, replica_groups=mesh['nodes'=64,'feat'=12] {'feat'}, dimensions={0}, use_global_device_ids=true | all-gather | bytes 638976 | tf_op jit(solution)/shard_map/all_gather | solution.py:62
  136.5 21.4 %all_gather.7 = bf16[1152,256]{1,0:T(8,128)(2,1)} all-gather(bf16[96,256]{1,0:T(8,128)(2,1)S(1)} %copy-done.2), channel_id=1, replica_groups=mesh['nodes'=64,'feat'=12] {'feat'}, dimensions={0}, use_global_device_ids=true | all-gather | bytes 638976 | tf_op jit(solution)/shard_map/all_gather | solution.py:63
  157.8 1.1 copy.35
  158.9 0.2 all_to_all.36
  159.1 0.1 copy.32
  159.3 0.2 all_to_all.32
  159.5 0.2 fusion.36
  159.7 0.0 copy-done.7
  159.7 2.0 convert_reduce_fusion
  161.7 1.4 fusion.37
  163.1 0.0 reduce-scatter.3.cloned.1.call-update
  163.1 0.0 reduce-scatter.5.cloned.1.call-start
  163.2 1.4 fusion.38
  164.5 0.0 reduce-scatter.5.cloned.1.call-update
  164.6 0.0 all-reduce.3.cloned.1.call-start
  164.6 54.5 %reduce-scatter.3.cloned.1.call-done = f32[96,256]{1,0:T(8,128)} async-done(((f32[1152,256]{1,0:T(8,128)}), f32[96,256]{1,0:T(8,128)}) %reduce-scatter.3.cloned.1.call-update) | async-done | bytes 98320 | tf_op jit(solution)/shard_map/reduce_scatter | solution.py:75
  219.1 60.1 %reduce-scatter.5.cloned.1.call-done = f32[96,256]{1,0:T(8,128)} async-done(((f32[1152,256]{1,0:T(8,128)}), f32[96,256]{1,0:T(8,128)}) %reduce-scatter.5.cloned.1.call-update) | async-done | bytes 98320 | tf_op jit(solution)/shard_map/reduce_scatter | solution.py:76
  279.2 0.0 all-reduce.3.cloned.1.call-update
  279.2 113.4 %psum.23 = f32[256]{0:T(256)} all-reduce(f32[256]{0:T(256)S(1)} %get-tuple-element.6), channel_id=1, replica_groups=mesh['nodes'=64,'feat'=12] {'nodes','feat'}, use_global_device_ids=true, to_apply=%region_5.6 | all-reduce | flops 256 | bytes 2048 | tf_op jit(solution)/shard_map/psum | solution.py:79
  392.6 94.3 %all-reduce.3.cloned.1.call-done = (f32[96,256]{1,0:T(8,128)}, f32[96,256]{1,0:T(8,128)}) async-done(((f32[96,256]{1,0:T(8,128)}, f32[96,256]{1,0:T(8,128)}), (f32[96,256]{1,0:T(8,128)}, f32[96,256]{1,0:T(8,128)})) %all-reduce.3.cloned.1.call-update) | async-done | bytes 196624 | tf_op jit(solution)/shard_map/psum | solution.py:78
  487.0 1.5 copy.42
  488.5 1.5 copy.43
  (26 shorter events, 0.1 us)
Async XLA Ops:
  7.2 3.7 copy-start
  15.0 15.5 %copy-start.3 = (s32[6,8]{1,0:T(8,128)S(1)}, s32[6,8]{1,0:T(8,128)}, u32[]{:S(2)}) copy-start(s32[6,8]{1,0:T(8,128)} %param.19) | copy-start | bytes 580
  15.0 54.6 %all-to-all-start = ((bf16[64,128,96]{1,2,0:T(8,128)(2,1)}), bf16[64,128,96]{1,2,0:T(8,128)(2,1)}, u32[]{:S(2)}, u32[]{:S(2)}) async-start(bf16[64,128,96]{1,2,0:T(8,128)(2,1)} %fusion.8), calls=%async_computation | async-start | bytes 3145728 | tf_op jit(solution)/shard_map/all_to_all | solution.py:39
  30.6 0.8 copy-start.4
  30.7 0.9 copy-start.9
  30.7 3.9 copy-start.10
  69.6 33.7 %all-to-all-start.2 = ((bf16[12,64,96]{2,1,0:T(8,128)(2,1)}), bf16[12,64,96]{2,1,0:T(8,128)(2,1)}, u32[]{:S(2)}, u32[]{:S(2)}) async-start(bf16[12,64,96]{2,1,0:T(8,128)(2,1)} %bitcast.12), calls=%async_computation.2 | async-start | bytes 393216 | tf_op jit(solution)/shard_map/all_to_all | solution.py:59
  94.1 3.9 copy-start.5
  98.0 1.9 copy-start.6
  101.3 11.1 %copy-start.1 = (bf16[96,256]{1,0:T(8,128)(2,1)S(1)}, bf16[96,256]{1,0:T(8,128)(2,1)}, u32[]{:S(2)}) copy-start(bf16[96,256]{1,0:T(8,128)(2,1)} %param.14) | copy-start | bytes 147460
  101.3 35.2 %copy-start.2 = (bf16[96,256]{1,0:T(8,128)(2,1)S(1)}, bf16[96,256]{1,0:T(8,128)(2,1)}, u32[]{:S(2)}) copy-start(bf16[96,256]{1,0:T(8,128)(2,1)} %param.15) | copy-start | bytes 147460
  103.3 55.8 %all-to-all-start.1 = ((bf16[12,64,96]{2,1,0:T(8,128)(2,1)}), bf16[12,64,96]{2,1,0:T(8,128)(2,1)S(1)}, u32[]{:S(2)}, u32[]{:S(2)}) async-start(bf16[12,64,96]{2,1,0:T(8,128)(2,1)} %divide_convert_fusion), calls=%async_computation.1 | async-start | bytes 393216 | tf_op jit(solution)/shard_map/all_to_all | solution.py:58
  112.3 106.7 %reduce-scatter.3.cloned.1.call-start = ((), (), s32[]{:S(2)}) async-start(), calls=%async_computation.5 | async-start | bytes 1277952 | tf_op jit(solution)/shard_map/reduce_scatter | solution.py:75
  136.5 23.3 %copy-start.7 = (bf16[64,256]{1,0:T(8,128)(2,1)S(1)}, bf16[64,256]{1,0:T(8,128)(2,1)}, u32[]{:S(2)}) copy-start(bf16[64,256]{1,0:T(8,128)(2,1)} %param.25) | copy-start | bytes 98308
  136.5 23.3 %copy-start.8 = (f32[256]{0:T(256)S(1)}, f32[256]{0:T(256)}, u32[]{:S(2)}) copy-start(f32[256]{0:T(256)} %param.16) | copy-start | bytes 3076
  163.1 116.1 %reduce-scatter.5.cloned.1.call-start = ((), (), s32[]{:S(2)}) async-start(), calls=%async_computation.6 | async-start | bytes 1277952 | tf_op jit(solution)/shard_map/reduce_scatter | solution.py:76
  164.6 322.4 %all-reduce.3.cloned.1.call-start = ((), (), s32[]{:S(2)}) async-start(), calls=%async_computation.7 | async-start | bytes 393216 | tf_op jit(solution)/shard_map/psum | solution.py:78
Sparse Core Ops, SparseCore 0:
  163.2 55.7 reduce-scatter.2
  222.5 56.6 reduce-scatter.4
  282.7 204.2 all-reduce.2
where the time goes:
time: 499 us; the launch traced here: 497 us
  waiting for transfers between devices  244 us (49%)
  blocking collectives  159 us (32%)
  starting transfers between devices  35.8 us (7%)
  local copies, waits for them, and re-layouts  30 us (6%)
  between operations  13.9 us (3%)
  matrix products  12.4 us (2%)
    psum x1, blocking collectives, local(): lax.psum(jnp.sum(slopes.astype(jnp.float32), axis=0), ('nodes', 'feat'))  113 us
    psum x1, waiting for transfers between devices, local(): grad_neigh, grad_self = lax.psum((grad_neigh, grad_self), 'nodes')  94.3 us
    reduce_scatter x1, waiting for transfers between devices, local(): lax.psum_scatter(self_terms, 'feat', scatter_dimension=0, tiled=True)  60.1 us
    reduce_scatter x1, waiting for transfers between devices, local(): lax.psum_scatter(neigh_terms, 'feat', scatter_dimension=0, tiled=True)  54.5 us
    all_to_all x1, waiting for transfers between devices, local(): lax.all_to_all(outgoing, 'nodes', split_axis=0, concat_axis=0, tiled=True)  35 us
    all_gather x1, blocking collectives, local(): lax.all_gather(w_neigh, 'feat', axis=0, tiled=True)  24.1 us
    all_gather x1, blocking collectives, local(): lax.all_gather(w_self, 'feat', axis=0, tiled=True)  21.4 us
    all_to_all x1, starting transfers between devices, local(): lax.all_to_all(outgoing, 'nodes', split_axis=0, concat_axis=0, tiled=True)  15.5 us
  transfers between devices with their start and end apart: 6, of which 4 were waited for; matrix products, arithmetic and copies ran while one was open for 6% of the time, Pallas kernels for 0%

commit v1 on v0

v1 whole, which is shorter than its diff:
```python
import functools

import jax
import jax.numpy as jnp
from jax import lax
from jax.experimental import pallas as pl
from jax.experimental.pallas import tpu as pltpu
from jax.sharding import PartitionSpec as P

BF = jnp.bfloat16
F32 = jnp.float32
MESH = pl.DeviceIdType.MESH
BLK = 128
HALF = 64
ROW_SIZE = 8


def dot_nt(a, b):
    return lax.dot_general(a, b, (((1,), (1,)), ((), ())), preferred_element_type=F32)


def dot_tn(a, b):
    return lax.dot_general(a, b, (((0,), (0,)), ((), ())), preferred_element_type=F32)


def loop(low, high, body):
    lax.fori_loop(low, high, lambda i, carry: (body(i), carry)[1], 0)


def pack_halves(block):
    mid = block.shape[0] // 2
    top, bottom = block[:mid], block[mid:]
    first = jnp.concatenate([top[:, :HALF], bottom[:, :HALF]], axis=1)
    second = jnp.concatenate([top[:, HALF:], bottom[:, HALF:]], axis=1)
    return first, second


def kernel(
    row,
    feat_hbm, wn_hbm, ws_hbm, bias_ref, tb, loct_hbm, lsrc, lcnt, remt_hbm, rsrc, rslot, deg_ref, cot_ref,
    act_ref, gn_ref, gs_ref, gb_ref,
    feat_v, xt, remt, loct, sb, rb, near, pacc, slot_v, slot_m, ring_out, ring_in,
    own_t, agg_t, own_s, own_r, agg_s, agg_r, wall, sl,
    ar_g, ar_r, ar_sum, ar_y, ar_t, ar_full,
    ld, ld_rem, row_ss, row_rs, slot_ss, slot_rs, ring_ss, ring_rs,
    own_ss, own_rs, agg_ss, agg_rs, w_ss, w_rs, wc_ss, wc_rs, sl_ss, sl_rs,
    a_ss, a_rs, b_ss, b_rs, c_ss, c_rs, d_ss, d_rs,
):
    n = lax.axis_index("nodes")
    z = lax.axis_index("feat")
    nodes = lax.axis_size("nodes")
    zs = lax.axis_size("feat")
    col = nodes // row
    reach = col // 2
    last = col - 1
    y = lax.div(n, row)
    g = lax.rem(n, row)
    core = lax.rem(g, 2)
    targets = near.shape[0]
    fw = xt.shape[1]
    mid = fw // 2
    nblocks = xt.shape[0]

    def row_peer(r):
        return y * row + lax.rem(g + r, row)

    def col_peer(k):
        return lax.rem(y + k, col) * row + g

    def z_peer(k):
        return lax.rem(z + k, zs)

    def delta(p):
        return (reach - (p + 1) // 2) * (2 * (p % 2) - 1)

    def to_node(src, dst, ssem, rsem, node):
        return pltpu.make_async_remote_copy(
            src_ref=src, dst_ref=dst, send_sem=ssem, recv_sem=rsem, device_id={"nodes": node}, device_id_type=MESH
        )

    def to_feat(src, dst, ssem, rsem, peer):
        return pltpu.make_async_remote_copy(
            src_ref=src, dst_ref=dst, send_sem=ssem, recv_sem=rsem, device_id={"feat": peer}, device_id_type=MESH
        )

    barrier = pltpu.get_barrier_semaphore()
    for r in range(1, row):
        pl.semaphore_signal(barrier, inc=1, device_id={"nodes": row_peer(r)}, device_id_type=MESH)
    for k in range(1, col):
        pl.semaphore_signal(barrier, inc=1, device_id={"nodes": col_peer(k)}, device_id_type=MESH)
    for k in range(1, zs):
        pl.semaphore_signal(barrier, inc=1, device_id={"feat": z_peer(k)}, device_id_type=MESH)

    load_feat = pltpu.make_async_copy(feat_hbm, feat_v, ld.at[0])
    load_feat.start()

    def dest_row(p):
        return lax.rem(y + delta(p) + col, col)

    def load_rem(p):
        return pltpu.make_async_copy(remt_hbm.at[0, pl.ds(dest_row(p) * row, row)], remt.at[p], ld_rem.at[p])

    for p in range(col):
        load_rem(p).start()
    load_loc = pltpu.make_async_copy(loct_hbm, loct, ld.at[1])
    load_loc.start()
    load_wn = pltpu.make_async_copy(wn_hbm, wall.at[0, z], ld.at[2])
    load_ws = pltpu.make_async_copy(ws_hbm, wall.at[1, z], ld.at[2])

    @pl.when(core == 0)
    def _():
        load_wn.start()

    @pl.when(core == 1)
    def _():
        load_ws.start()

    slot_v[0] = jnp.zeros(slot_v.shape[1:], jnp.int32)
    slot_v[0, 0:1, 0:nodes] = rslot[...]

    load_feat.wait()
    for b in range(nblocks):
        xt[b] = feat_v[b * BLK : (b + 1) * BLK, :].astype(F32).T.astype(BF)
    for j in range(targets):
        block = xt[tb[j]]
        own_t[j] = block
        first, second = pack_halves(block)
        own_s[2 * j] = first
        own_s[2 * j + 1] = second
    own_r[z] = own_s[z]

    def messages(p):
        load_rem(p).wait()
        yd = dest_row(p)
        for r in range(row):
            gd = lax.rem(g + r, row)
            block = xt[rsrc[0, yd * row + gd]]
            message = dot_nt(block, remt[p, gd]).astype(BF)
            if r == 0:
                rb[0, p] = message
            else:
                sb[r, p] = message

    def row_copy(r, p):
        return to_node(sb.at[r, p], rb.at[r, p], row_ss.at[r, p], row_rs.at[r, p], row_peer(r))

    messages(0)
    pl.semaphore_wait(barrier, row + col + zs - 3)

    def slot_copy(k):
        return to_node(slot_v.at[0], slot_v.at[k], slot_ss.at[k], slot_rs.at[k], col_peer(k))

    def own_copy(k):
        return to_feat(own_s.at[z_peer(k)], own_r.at[z], own_ss.at[k], own_rs.at[k], z_peer(k))

    def w_copy(k):
        return to_feat(wall.at[core, z], wall.at[core, z], w_ss.at[k], w_rs.at[k], z_peer(k))

    for r in range(1, row):
        row_copy(r, 0).start()
    for k in range(1, col):
        slot_copy(k).start()

    @pl.when(core == 0)
    def _():
        load_wn.wait()

    @pl.when(core == 1)
    def _():
        load_ws.wait()

    for k in range(1, zs):
        w_copy(k).start()

    def more(p):
        messages(p)
        for r in range(1, row):
            row_copy(r, p).start()

    loop(1, col, more)
    for k in range(1, zs):
        own_copy(k).start()

    load_loc.wait()

    def nearby(t):
        total = jnp.zeros((fw, BLK), F32)
        for k in range(lsrc.shape[1]):
            block = xt[lsrc[t, k]]
            block = jnp.where(k < lcnt[t], block, jnp.zeros_like(block))
            total = total + dot_nt(block, loct[t, k])
        near[t] = total

    loop(0, targets, nearby)

    for k in range(1, col):
        slot_copy(k).wait_recv()
    slots = pltpu.make_async_copy(slot_v, slot_m, ld.at[3])
    slots.start()
    slots.wait()

    def collapse(p, j, start):
        k = lax.rem(col - delta(p), col)
        total = start
        for r in range(row):
            source = y * row + lax.rem(g - r + row, row)
            hit = slot_m[k, 0, source] == j
            message = rb[r, p].astype(F32)
            total = total + jnp.where(hit, message, jnp.zeros_like(message))
        return total

    def row_wait(p):
        for r in range(1, row):
            row_copy(r, p).wait_recv()

    up = lax.rem(y + 1, col) * row + g
    down = lax.rem(y + col - 1, col) * row + g
    sides = (up, down)

    def ring_first(side):
        rows = pl.ds(side * mid, mid)
        return to_node(
            ring_out.at[0, :, rows], ring_in.at[side, 0, :, rows], ring_ss.at[side, 0], ring_rs.at[side, 0], sides[side]
        )

    def ring_copy(p):
        side, step = (p - 1) % 2, (p - 1) // 2 + 1
        return to_node(
            ring_out.at[p], ring_in.at[side, step], ring_ss.at[side, step], ring_rs.at[side, step], sides[side]
        )

    def ring_wait(side, step):
        if step == 0:
            ring_first(side).wait_recv()
        else:
            ring_copy(2 * step - 1 + side).wait_recv()

    row_wait(0)

    def start_ring(j):
        ring_out[0, j] = collapse(0, j, jnp.zeros((fw, BLK), F32)).astype(BF)

    loop(0, targets, start_ring)
    ring_first(0).start()
    ring_first(1).start()

    for p in range(1, last):
        side, step = (p - 1) % 2, (p - 1) // 2
        row_wait(p)

        def partial(j, p=p):
            pacc[j] = collapse(p, j, jnp.zeros((fw, BLK), F32))

        loop(0, targets, partial)
        ring_wait(side, step)

        def merge(j, p=p, side=side, step=step):
            if step == 0:
                own = pl.ds(side * mid, mid)
                other = pl.ds((1 - side) * mid, mid)
                ring_out[p, j, own] = (pacc[j, own] + ring_in[side, 0, j, own].astype(F32)).astype(BF)
                ring_out[p, j, other] = pacc[j, other].astype(BF)
            else:
                ring_out[p, j] = (pacc[j] + ring_in[side, step, j].astype(F32)).astype(BF)

        loop(0, targets, merge)
        ring_copy(p).start()

    partner = n + 1 - 2 * core

    def w_hand():
        return to_node(wall.at[core], wall.at[core], wc_ss.at[0], wc_rs.at[0], partner)

    def w_take():
        return to_node(wall.at[1 - core], wall.at[1 - core], wc_ss.at[0], wc_rs.at[0], partner)

    for k in range(1, zs):
        w_copy(k).wait_recv()
    w_hand().start()

    row_wait(last)

    def finish(j):
        near[j] = collapse(last, j, near[j])

    loop(0, targets, finish)

    for k in range(1, zs):
        own_copy(k).wait_recv()
    w_take().wait_recv()

    def project(pieces, which):
        width = wall.shape[-1]
        flat = pieces[...].reshape(zs * mid, BLK)
        first = wall[which, :, :mid, :].reshape(zs * mid, width)
        second = wall[which, :, mid:, :].reshape(zs * mid, width)
        return dot_tn(flat, first)[:HALF] + dot_tn(flat, second)[HALF:]

    self_part = project(own_r, 1) + bias_ref[...].reshape(1, -1)

    ring_wait(0, reach - 1)
    ring_wait(1, reach - 1)

    def agg_copy(dest):
        return to_feat(agg_s.at[dest], agg_r.at[z], agg_ss.at[dest], agg_rs.at[z], dest)

    for j in range(targets):
        total = near[j] + ring_in[0, reach - 1, j].astype(F32) + ring_in[1, reach - 1, j].astype(F32)
        degree = deg_ref[pl.ds(j * BLK, BLK)].reshape(1, BLK).astype(F32)
        block = (total / degree).astype(BF)
        agg_t[j] = block
        first, second = pack_halves(block)
        for half, piece in ((0, first), (1, second)):
            dest = 2 * j + half
            agg_s[dest] = piece

            @pl.when(z != dest)
            def _(dest=dest):
                agg_copy(dest).start()

            @pl.when(z == dest)
            def _(dest=dest, piece=piece):
                agg_r[dest] = piece

    def agg_wait(k):
        source = z_peer(k)
        to_feat(agg_s.at[source], agg_r.at[source], agg_ss.at[source], agg_rs.at[source], source).wait_recv()

    for k in range(1, zs):
        agg_wait(k)
    pre = project(agg_r, 0) + self_part

    scale = 0.7978845608028654
    cubic = 0.044715
    inner = jnp.tanh(scale * (pre + cubic * (pre * pre * pre)))
    cdf = 0.5 * (1.0 + inner)
    act_ref[...] = (pre * cdf).astype(BF)
    slope = cdf + pre * (0.5 * (1.0 - inner * inner)) * (scale * (1.0 + 3.0 * cubic * (pre * pre)))
    sl[z] = (cot_ref[...].astype(F32) * slope).astype(BF)

    def sl_copy(k):
        return to_feat(sl.at[z], sl.at[z], sl_ss.at[k], sl_rs.at[k], z_peer(k))

    for k in range(1, zs):
        sl_copy(k).start()
    for k in range(1, zs):
        sl_copy(k).wait_recv()

    width = sl.shape[-1]
    grad_n = jnp.zeros((fw, width), F32)
    grad_s = jnp.zeros((fw, width), F32)
    grad_b = jnp.zeros((8, width), F32)
    for j in range(targets):
        rows = sl[2 * j : 2 * j + 2].reshape(BLK, width)
        grad_n = grad_n + jnp.dot(agg_t[j], rows, preferred_element_type=F32)
        grad_s = grad_s + jnp.dot(own_t[j], rows, preferred_element_type=F32)
        grad_b = grad_b + rows.astype(F32).reshape(BLK // 8, 8, width).sum(axis=0)
    per = 4 * fw // row
    unit = mid
    share = ar_t.shape[0] // col

    def places():
        for u in range(8):
            yield u // 4, (u // 2) % 2, u % 2, u * unit // per, u * unit % per

    for which, side, part, owner, at in places():
        grad = (grad_n, grad_s)[which]
        ar_g[owner, at : at + unit] = grad[part * unit : (part + 1) * unit, side * BLK : (side + 1) * BLK]
    for owner in range(row):
        ar_g[owner, per : per + 8] = grad_b[:, :BLK]
        ar_g[owner, per + 8 : per + 16] = grad_b[:, BLK:]
        if ar_t.shape[0] > per + 16:
            ar_g[owner, per + 16 :] = jnp.zeros((ar_t.shape[0] - per - 16, BLK), F32)

    def a_copy(r):
        return to_node(ar_g.at[lax.rem(g + r, row)], ar_r.at[r], a_ss.at[r], a_rs.at[r], row_peer(r))

    for r in range(1, row):
        a_copy(r).start()
    total = ar_g[g]
    for r in range(1, row):
        a_copy(r).wait_recv()
        total = total + ar_r[r]
    ar_sum[...] = total

    def b_copy(k):
        rows = pl.ds(pl.multiple_of(lax.rem(y + k, col) * share, 8), share)
        return to_node(ar_sum.at[rows], ar_y.at[k], b_ss.at[k], b_rs.at[k], col_peer(k))

    for k in range(1, col):
        b_copy(k).start()
    mine = pl.ds(pl.multiple_of(y * share, 8), share)
    total = ar_sum[mine]
    for k in range(1, col):
        b_copy(k).wait_recv()
        total = total + ar_y[k]
    ar_t[mine] = total

    def c_copy(k):
        return to_node(ar_t.at[mine], ar_t.at[mine], c_ss.at[k], c_rs.at[k], col_peer(k))

    for k in range(1, col):
        c_copy(k).start()
    for k in range(1, col):
        c_copy(k).wait_recv()

    def d_copy(r):
        return to_node(ar_t, ar_full.at[g], d_ss.at[r], d_rs.at[r], row_peer(r))

    for r in range(1, row):
        d_copy(r).start()
    ar_full[g] = ar_t[...]
    for r in range(1, row):
        d_copy(r).wait_recv()

    for which, side, part, owner, at in places():
        out = (gn_ref, gs_ref)[which]
        out[part * unit : (part + 1) * unit, side * BLK : (side + 1) * BLK] = ar_full[owner, at : at + unit]
    gb_ref[:, :BLK] = ar_full[0, per : per + 8].sum(axis=0, keepdims=True)
    gb_ref[:, BLK:] = ar_full[0, per + 8 : per + 16].sum(axis=0, keepdims=True)

    def row_sent(p):
        for r in range(1, row):
            row_copy(r, p).wait_send()

    loop(0, col, row_sent)
    for side in range(2):
        ring_first(side).wait_send()
    for p in range(1, last):
        ring_copy(p).wait_send()
    w_hand().wait_send()
    for k in range(1, col):
        slot_copy(k).wait_send()
        b_copy(k).wait_send()
        c_copy(k).wait_send()
    for r in range(1, row):
        a_copy(r).wait_send()
        d_copy(r).wait_send()
    for k in range(1, zs):
        own_copy(k).wait_send()
        w_copy(k).wait_send()
        sl_copy(k).wait_send()
        agg_copy(z_peer(k)).wait_send()


def local(row, features, w_neigh, w_self, bias, target_blocks, loc_tiles, loc_src, loc_count, rem_tiles, rem_src,
          rem_slot, degree, cotangent):
    fw = features.shape[1]
    nblocks = features.shape[0] // BLK
    targets, slots = loc_src.shape
    nodes = lax.axis_size("nodes")
    zs = lax.axis_size("feat")
    col = nodes // row
    width = w_neigh.shape[1]
    mid = fw // 2
    per = 4 * fw // row
    chunk = -(-(per + 16) // (8 * col)) * 8 * col
    hbm = pl.BlockSpec(memory_space=pl.ANY)
    vmem = pl.BlockSpec(memory_space=pltpu.VMEM)
    smem = pl.BlockSpec(memory_space=pltpu.SMEM)
    dma = pltpu.SemaphoreType.DMA
    scratch = [
        pltpu.VMEM(features.shape, BF),
        pltpu.VMEM((nblocks, fw, BLK), BF),
        pltpu.VMEM((col, row, BLK, BLK), BF),
        pltpu.VMEM((targets, slots, BLK, BLK), BF),
        pltpu.VMEM((row, col, fw, BLK), BF),
        pltpu.VMEM((row, col, fw, BLK), BF),
        pltpu.VMEM((targets, fw, BLK), F32),
        pltpu.VMEM((targets, fw, BLK), F32),
        pltpu.VMEM((col, 8, BLK), jnp.int32),
        pltpu.SMEM((col, 8, BLK), jnp.int32),
        pltpu.VMEM((col - 1, targets, fw, BLK), BF),
        pltpu.VMEM((2, col // 2, targets, fw, BLK), BF),
        pltpu.VMEM((targets, fw, BLK), BF),
        pltpu.VMEM((targets, fw, BLK), BF),
        pltpu.VMEM((zs, mid, BLK), BF),
        pltpu.VMEM((zs, mid, BLK), BF),
        pltpu.VMEM((zs, mid, BLK), BF),
        pltpu.VMEM((zs, mid, BLK), BF),
        pltpu.VMEM((2, zs, fw, width), BF),
        pltpu.VMEM((zs, HALF, width), BF),
        pltpu.VMEM((row, chunk, BLK), F32),
        pltpu.VMEM((row, chunk, BLK), F32),
        pltpu.VMEM((chunk, BLK), F32),
        pltpu.VMEM((col, chunk // col, BLK), F32),
        pltpu.VMEM((chunk, BLK), F32),
        pltpu.VMEM((row, chunk, BLK), F32),
        dma((4,)), dma((col,)),
        dma((row, col)), dma((row, col)),
        dma((col,)), dma((col,)),
        dma((2, col // 2)), dma((2, col // 2)),
        dma((zs,)), dma((zs,)),
        dma((zs,)), dma((zs,)),
        dma((zs,)), dma((zs,)),
        dma((1,)), dma((1,)),
        dma((zs,)), dma((zs,)),
        dma((row,)), dma((row,)),
        dma((col,)), dma((col,)),
        dma((col,)), dma((col,)),
        dma((row,)), dma((row,)),
    ]
    activation, grad_neigh, grad_self, grad_bias = pl.pallas_call(
        functools.partial(kernel, row),
        out_shape=(
            jax.ShapeDtypeStruct(cotangent.shape, BF),
            jax.ShapeDtypeStruct(w_neigh.shape, F32),
            jax.ShapeDtypeStruct(w_self.shape, F32),
            jax.ShapeDtypeStruct((1, width), F32),
        ),
        in_specs=[hbm, hbm, hbm, vmem, smem, hbm, smem, smem, hbm, smem, vmem, vmem, vmem],
        out_specs=(vmem, vmem, vmem, vmem),
        scratch_shapes=scratch,
        compiler_params=pltpu.CompilerParams(
            collective_id=0, has_side_effects=True, vmem_limit_bytes=40 * 1024 * 1024
        ),
        name="sage_layer",
    )(features, w_neigh, w_self, bias, target_blocks, loc_tiles, loc_src, loc_count, rem_tiles, rem_src, rem_slot,
      degree, cotangent)
    return activation, grad_neigh, grad_self, grad_bias.reshape(width)


def solution(mesh, row=ROW_SIZE):
    return jax.shard_map(
        functools.partial(local, row),
        mesh=mesh,
        in_specs=(
            P("nodes", "feat"),
            P("feat", None),
            P("feat", None),
            P(),
            P("nodes"),
            P("nodes", None, None, None),
            P("nodes", None),
            P("nodes"),
            P("nodes", None, None, None),
            P("nodes", None),
            P("nodes", None),
            P("nodes"),
            P(("nodes", "feat"), None),
        ),
        out_specs=(P(("nodes", "feat"), None), P("feat", None), P("feat", None), P()),
        check_vma=False,
    )
```

time: 499 us -> 108 us (0.22)
  waiting for transfers between devices: 244 us -> 0 us
  blocking collectives: 159 us -> 0 us
  Pallas kernels: 0 us -> 93.3 us
  starting transfers between devices: 35.8 us -> 0 us
  local copies, waits for them, and re-layouts: 30 us -> 13.6 us
  between operations: 13.9 us -> 0.67 us
  matrix products: 12.4 us -> 0 us
    reduce_scatter x2 -> x0, waiting for transfers between devices: 115 us -> none  [the longest x1 60.1 us: local(): lax.psum_scatter(self_terms, 'feat', scatter_dimension=0, tiled=True)]
    psum x1 -> x0, blocking collectives: 113 us -> none  [local(): lax.psum(jnp.sum(slopes.astype(jnp.float32), axis=0), ('nodes', 'feat'))]
    psum x1 -> x0, waiting for transfers between devices: 94.3 us -> none  [local(): grad_neigh, grad_self = lax.psum((grad_neigh, grad_self), 'nodes')]
    pallas_call x0 -> x1, Pallas kernels: none -> 93.3 us  [local(): pl.pallas_call(functools.partial(kernel, row), out_shape=(jax.ShapeDtypeS...]
    all_gather x2 -> x0, blocking collectives: 45.4 us -> none  [the longest x1 24.1 us: local(): lax.all_gather(w_neigh, 'feat', axis=0, tiled=True)]
    all_to_all x3 -> x0, starting transfers between devices: 35.7 us -> none  [the longest x1 15.5 us: local(): lax.all_to_all(outgoing, 'nodes', split_axis=0, concat_axis=0, tiled=True)]
    all_to_all x3 -> x0, waiting for transfers between devices: 35 us -> none  [the longest x1 35 us: local(): lax.all_to_all(outgoing, 'nodes', split_axis=0, concat_axis=0, tiled=True)]
    dot_general x7 -> x0, matrix products: 12.4 us -> none  [the longest x1 4.14 us: local(): jnp.einsum('dij,djf->dif', rem_tiles[0], chosen, preferred_element_type=j...]
  transfers between devices with their start and end apart: 6 -> 0, of which waited for: 4 -> 0; matrix products, arithmetic and copies ran while one was open for 6% -> 0% of each run, Pallas kernels for 0% -> 0%
where the time goes in v1:
time: 108 us
  Pallas kernels  93.3 us (86%)
  local copies, waits for them, and re-layouts  13.6 us (13%)
    pallas_call x1, Pallas kernels, local(): pl.pallas_call(functools.partial(kernel, row), out_shape=(jax.ShapeDtypeS...  93.3 us
    unnamed x29, local copies, waits for them, and re-layouts  13.6 us

profile of v1, /device:TPU:1, one launch (start us, length us, event | category | flops | bytes accessed | tf_op | source)
XLA Modules:
  0.0 107.5 jit_solution(11184585703656511138)
XLA Ops:
  0.6 1.1 %copy.17.feat_hbm = bf16[1024,96]{1,0:T(8,128)(2,1)S(1)} copy(bf16[1024,96]{0,1:T(8,128)(2,1)} %param.13) | data formatting | bytes 393216 | tf_op args[0]
  1.7 0.0 copy-start
  1.7 1.6 %copy-done = bf16[1,64,128,128]{3,2,1,0:T(8,128)(2,1)S(1)} copy-done((bf16[1,64,128,128]{3,2,1,0:T(8,128)(2,1)S(1)}, bf16[1,64,128,128]{3,2,1,0:T(8,128)(2,1)}, u32[]{:S(2)}) %copy-start) | copy-done | bytes 2097176
  3.3 0.0 copy-start.1
  3.3 1.4 %copy-done.1 = bf16[6,8,128,128]{3,2,1,0:T(8,128)(2,1)S(1)} copy-done((bf16[6,8,128,128]{3,2,1,0:T(8,128)(2,1)S(1)}, bf16[6,8,128,128]{3,2,1,0:T(8,128)(2,1)}, u32[]{:S(2)}) %copy-start.1) | copy-done | bytes 1572888
  4.7 0.0 copy-start.2
  4.7 0.8 copy-done.2
  5.5 0.0 copy-start.3
  5.5 0.8 copy-done.3
  6.3 0.0 copy-start.4
  6.3 0.8 copy-done.4
  7.1 0.0 copy-start.5
  7.1 0.7 copy-done.5
  7.8 0.0 copy-start.6
  7.8 0.7 copy-done.6
  8.5 0.0 copy-start.7
  8.5 0.7 copy-done.7
  9.1 0.0 copy-start.8
  9.1 0.7 copy-done.8
  9.8 0.0 copy-start.9
  9.8 0.7 copy-done.9
  10.5 0.0 copy-start.10
  10.5 0.7 copy-done.10
  11.1 0.0 copy-start.11
  11.1 0.7 copy-done.11
  11.8 93.3 %sage_layer.1 = (bf16[64,256]{1,0:T(8,128)(2,1)S(1)}, f32[96,256]{1,0:T(8,128)S(1)}, f32[96,256]{1,0:T(8,128)S(1)}, f32[1,256]{1,0:T(1,128)S(1)}) custom-call(bf16[1024,96]{1,0:T(8,128)(2,1)S(1)} %copy.17.feat_hbm, bf16[96,256]{1,0:T(8,128)(2,1)S(1)} %copy-done.2, bf16[96,256]{1,0:T(8,128)(2,1)S(1)} %copy-done.3, f32[256]{0:T(256)S(1)} %copy-done.7, ...), custom_call_target="tpu_custom_call" | custom-call | tf_op jit(solution)/shard_map/sage_layer/pallas_call | solution.py:503
  105.1 0.6 copy.22
  105.7 0.6 copy.23
  106.3 0.6 copy.24
  107.0 0.6 copy.25
Async XLA Ops:
  1.7 1.6 %copy-start = (bf16[1,64,128,128]{3,2,1,0:T(8,128)(2,1)S(1)}, bf16[1,64,128,128]{3,2,1,0:T(8,128)(2,1)}, u32[]{:S(2)}) copy-start(bf16[1,64,128,128]{3,2,1,0:T(8,128)(2,1)} %remt_hbm.1) | copy-start | bytes 6291460
  3.3 1.4 %copy-start.1 = (bf16[6,8,128,128]{3,2,1,0:T(8,128)(2,1)S(1)}, bf16[6,8,128,128]{3,2,1,0:T(8,128)(2,1)}, u32[]{:S(2)}) copy-start(bf16[6,8,128,128]{3,2,1,0:T(8,128)(2,1)} %loct_hbm.1) | copy-start | bytes 4718596
  4.7 0.8 copy-start.2
  5.5 0.8 copy-start.3
  6.3 0.8 copy-start.4
  7.1 0.7 copy-start.5
  7.8 0.7 copy-start.6
  8.5 0.7 copy-start.7
  9.1 0.7 copy-start.8
  9.8 0.7 copy-start.9
  10.5 0.7 copy-start.10
  11.1 0.7 copy-start.11

commit v2 on v1

--- a/solution.py
+++ b/solution.py
@@ -12,6 +12,7 @@
 MESH = pl.DeviceIdType.MESH
 BLK = 128
 HALF = 64
+SLOPE_PHASES = (3, 3)
 ROW_SIZE = 8
 
 
@@ -37,14 +38,15 @@
 
 def kernel(
     row,
-    feat_hbm, wn_hbm, ws_hbm, bias_ref, tb, loct_hbm, lsrc, lcnt, remt_hbm, rsrc, rslot, deg_ref, cot_ref,
-    act_ref, gn_ref, gs_ref, gb_ref,
-    feat_v, xt, remt, loct, sb, rb, near, pacc, slot_v, slot_m, ring_out, ring_in,
+    feat_hbm, wn_hbm, ws_hbm, bias_hbm, tb_hbm, loct_hbm, lsrc_hbm, lcnt_hbm, remt_hbm, rsrc_hbm, rslot_hbm, deg_hbm, cot_hbm,
+    act_ref, full_ref,
+    bias_ref, tb, lsrc, lcnt, rsrc, rslot, deg_ref, cot_ref,
+    xt, remt, loct, sb, rb, near, pacc, slot_v, slot_m, ring_out, ring_in,
     own_t, agg_t, own_s, own_r, agg_s, agg_r, wall, sl,
-    ar_g, ar_r, ar_sum, ar_y, ar_t, ar_full,
-    ld, ld_rem, row_ss, row_rs, slot_ss, slot_rs, ring_ss, ring_rs,
+    ar_g, ar_r, ar_y, ar_full,
+    ld, ld_small, ld_feat, ld_rem, row_ss, row_rs, slot_ss, slot_rs, ring_ss, ring_rs,
     own_ss, own_rs, agg_ss, agg_rs, w_ss, w_rs, wc_ss, wc_rs, sl_ss, sl_rs,
-    a_ss, a_rs, b_ss, b_rs, c_ss, c_rs, d_ss, d_rs,
+    a_ss, a_rs, b_ss, b_rs, d_ss, d_rs,
 ):
     n = lax.axis_index("nodes")
     z = lax.axis_index("feat")
@@ -83,6 +85,41 @@
             src_ref=src, dst_ref=dst, send_sem=ssem, recv_sem=rsem, device_id={"feat": peer}, device_id_type=MESH
         )
 
+    def relay(buffer, rows, reaches, ssem, rsem):
+        half = rows // 2
+        base, phases = 0, []
+        for reach_now in reaches:
+            top = min(base + reach_now, zs // 2)
+            phases.append((base, top))
+            base = top
+
+        def copy(side, dist, start):
+            sign = 1 - 2 * side
+            shard = lax.rem(z - sign * start + zs, zs)
+            peer = lax.rem(z + sign * (dist - start) + zs, zs)
+            part = pl.ds(side * half, half) if 2 * dist == zs else pl.ds(0, rows)
+            ref = buffer.at[shard, part]
+            return to_feat(ref, ref, ssem.at[side, dist], rsem.at[side, dist], peer)
+
+        def phase(i):
+            low, top = phases[i]
+            for side in range(2):
+                if low > 0:
+                    copy(side, low, phases[i - 1][0]).wait_recv()
+                for dist in range(top, low, -1):
+                    copy(side, dist, low).start()
+
+        def rest(wait_send):
+            for low, top in phases:
+                for dist in range(low + 1, top + 1):
+                    for side in range(2):
+                        if wait_send:
+                            copy(side, dist, low).wait_send()
+                        elif dist < top or dist == zs // 2:
+                            copy(side, dist, low).wait_recv()
+
+        return phase, rest
+
     barrier = pltpu.get_barrier_semaphore()
     for r in range(1, row):
         pl.semaphore_signal(barrier, inc=1, device_id={"nodes": row_peer(r)}, device_id_type=MESH)
@@ -91,8 +128,19 @@
     for k in range(1, zs):
         pl.semaphore_signal(barrier, inc=1, device_id={"feat": z_peer(k)}, device_id_type=MESH)
 
-    load_feat = pltpu.make_async_copy(feat_hbm, feat_v, ld.at[0])
-    load_feat.start()
+    def load_feat(b):
+        return pltpu.make_async_copy(feat_hbm.at[:, pl.ds(b * BLK, BLK)], xt.at[b], ld_feat.at[b])
+
+    small = [
+        pltpu.make_async_copy(src, dst, ld_small.at[i])
+        for i, (src, dst) in enumerate(
+            ((rsrc_hbm, rsrc), (tb_hbm, tb), (lsrc_hbm, lsrc), (lcnt_hbm, lcnt), (rslot_hbm, rslot), (deg_hbm, deg_ref),
+             (cot_hbm, cot_ref), (bias_hbm, bias_ref))
+        )
+    ]
+    small[0].start()
+    for b in range(nblocks):
+        load_feat(b).start()
 
     def dest_row(p):
         return lax.rem(y + delta(p) + col, col)
@@ -102,6 +150,8 @@
 
     for p in range(col):
         load_rem(p).start()
+    for copy in small[1:]:
+        copy.start()
     load_loc = pltpu.make_async_copy(loct_hbm, loct, ld.at[1])
     load_loc.start()
     load_wn = pltpu.make_async_copy(wn_hbm, wall.at[0, z], ld.at[2])
@@ -115,19 +165,9 @@
     def _():
         load_ws.start()
 
-    slot_v[0] = jnp.zeros(slot_v.shape[1:], jnp.int32)
-    slot_v[0, 0:1, 0:nodes] = rslot[...]
-
-    load_feat.wait()
+    small[0].wait()
     for b in range(nblocks):
-        xt[b] = feat_v[b * BLK : (b + 1) * BLK, :].astype(F32).T.astype(BF)
-    for j in range(targets):
-        block = xt[tb[j]]
-        own_t[j] = block
-        first, second = pack_halves(block)
-        own_s[2 * j] = first
-        own_s[2 * j + 1] = second
-    own_r[z] = own_s[z]
+        load_feat(b).wait()
 
     def messages(p):
         load_rem(p).wait()
@@ -145,6 +185,9 @@
         return to_node(sb.at[r, p], rb.at[r, p], row_ss.at[r, p], row_rs.at[r, p], row_peer(r))
 
     messages(0)
+    slot_v[0] = jnp.zeros(slot_v.shape[1:], jnp.int32)
+    small[4].wait()
+    slot_v[0, 0:1, 0:nodes] = rslot[...]
     pl.semaphore_wait(barrier, row + col + zs - 3)
 
     def slot_copy(k):
@@ -153,8 +196,7 @@
     def own_copy(k):
         return to_feat(own_s.at[z_peer(k)], own_r.at[z], own_ss.at[k], own_rs.at[k], z_peer(k))
 
-    def w_copy(k):
-        return to_feat(wall.at[core, z], wall.at[core, z], w_ss.at[k], w_rs.at[k], z_peer(k))
+    w_phase, w_rest = relay(wall.at[core], fw, (3, 3), w_ss, w_rs)
 
     for r in range(1, row):
         row_copy(r, 0).start()
@@ -169,8 +211,7 @@
     def _():
         load_ws.wait()
 
-    for k in range(1, zs):
-        w_copy(k).start()
+    w_phase(0)
 
     def more(p):
         messages(p)
@@ -178,6 +219,16 @@
             row_copy(r, p).start()
 
     loop(1, col, more)
+
+    for copy in small[1:4] + small[5:]:
+        copy.wait()
+    for j in range(targets):
+        block = xt[tb[j]]
+        own_t[j] = block
+        first, second = pack_halves(block)
+        own_s[2 * j] = first
+        own_s[2 * j + 1] = second
+    own_r[z] = own_s[z]
     for k in range(1, zs):
         own_copy(k).start()
 
@@ -192,6 +243,7 @@
         near[t] = total
 
     loop(0, targets, nearby)
+
 
     for k in range(1, col):
         slot_copy(k).wait_recv()
@@ -265,6 +317,8 @@
 
         loop(0, targets, merge)
         ring_copy(p).start()
+        if p == 2 and zs > 6:
+            w_phase(1)
 
     partner = n + 1 - 2 * core
 
@@ -274,8 +328,7 @@
     def w_take():
         return to_node(wall.at[1 - core], wall.at[1 - core], wc_ss.at[0], wc_rs.at[0], partner)
 
-    for k in range(1, zs):
-        w_copy(k).wait_recv()
+    w_rest(False)
     w_hand().start()
 
     row_wait(last)
@@ -338,13 +391,12 @@
     slope = cdf + pre * (0.5 * (1.0 - inner * inner)) * (scale * (1.0 + 3.0 * cubic * (pre * pre)))
     sl[z] = (cot_ref[...].astype(F32) * slope).astype(BF)
 
-    def sl_copy(k):
-        return to_feat(sl.at[z], sl.at[z], sl_ss.at[k], sl_rs.at[k], z_peer(k))
-
-    for k in range(1, zs):
-        sl_copy(k).start()
-    for k in range(1, zs):
-        sl_copy(k).wait_recv()
+    sl_phase, sl_rest = relay(sl, HALF, SLOPE_PHASES, sl_ss, sl_rs)
+    sl_phase(0)
+    for i in range(1, len(SLOPE_PHASES)):
+        if sum(SLOPE_PHASES[:i]) < zs // 2:
+            sl_phase(i)
+    sl_rest(False)
 
     width = sl.shape[-1]
     grad_n = jnp.zeros((fw, width), F32)
@@ -356,68 +408,45 @@
         grad_s = grad_s + jnp.dot(own_t[j], rows, preferred_element_type=F32)
         grad_b = grad_b + rows.astype(F32).reshape(BLK // 8, 8, width).sum(axis=0)
     per = 4 * fw // row
-    unit = mid
-    share = ar_t.shape[0] // col
-
-    def places():
-        for u in range(8):
-            yield u // 4, (u // 2) % 2, u % 2, u * unit // per, u * unit % per
-
-    for which, side, part, owner, at in places():
+    for which, side, part, owner, at in places(row, fw):
+        unit = fw // 2
         grad = (grad_n, grad_s)[which]
-        ar_g[owner, at : at + unit] = grad[part * unit : (part + 1) * unit, side * BLK : (side + 1) * BLK]
+        ar_g[owner, at : at + unit] = grad[part * unit : (part + 1) * unit, side * BLK : (side + 1) * BLK].astype(BF)
+    bias_part = jnp.concatenate([grad_b[:, :BLK], grad_b[:, BLK:]], axis=0).astype(BF)
     for owner in range(row):
-        ar_g[owner, per : per + 8] = grad_b[:, :BLK]
-        ar_g[owner, per + 8 : per + 16] = grad_b[:, BLK:]
-        if ar_t.shape[0] > per + 16:
-            ar_g[owner, per + 16 :] = jnp.zeros((ar_t.shape[0] - per - 16, BLK), F32)
+        ar_g[owner, per : per + 16] = bias_part
 
     def a_copy(r):
         return to_node(ar_g.at[lax.rem(g + r, row)], ar_r.at[r], a_ss.at[r], a_rs.at[r], row_peer(r))
 
     for r in range(1, row):
         a_copy(r).start()
-    total = ar_g[g]
+    total = ar_g[g].astype(F32)
     for r in range(1, row):
         a_copy(r).wait_recv()
-        total = total + ar_r[r]
-    ar_sum[...] = total
+        total = total + ar_r[r].astype(F32)
+    ar_y[y] = total.astype(BF)
 
     def b_copy(k):
-        rows = pl.ds(pl.multiple_of(lax.rem(y + k, col) * share, 8), share)
-        return to_node(ar_sum.at[rows], ar_y.at[k], b_ss.at[k], b_rs.at[k], col_peer(k))
+        return to_node(ar_y.at[y], ar_y.at[y], b_ss.at[k], b_rs.at[k], col_peer(k))
 
     for k in range(1, col):
         b_copy(k).start()
-    mine = pl.ds(pl.multiple_of(y * share, 8), share)
-    total = ar_sum[mine]
     for k in range(1, col):
         b_copy(k).wait_recv()
-        total = total + ar_y[k]
-    ar_t[mine] = total
-
-    def c_copy(k):
-        return to_node(ar_t.at[mine], ar_t.at[mine], c_ss.at[k], c_rs.at[k], col_peer(k))
-
+    total = ar_y[0].astype(F32)
     for k in range(1, col):
-        c_copy(k).start()
-    for k in range(1, col):
-        c_copy(k).wait_recv()
+        total = total + ar_y[k].astype(F32)
+    ar_full[g] = total.astype(BF)
 
     def d_copy(r):
-        return to_node(ar_t, ar_full.at[g], d_ss.at[r], d_rs.at[r], row_peer(r))
+        return to_node(ar_full.at[g], ar_full.at[g], d_ss.at[r], d_rs.at[r], row_peer(r))
 
     for r in range(1, row):
         d_copy(r).start()
-    ar_full[g] = ar_t[...]
     for r in range(1, row):
         d_copy(r).wait_recv()
-
-    for which, side, part, owner, at in places():
-        out = (gn_ref, gs_ref)[which]
-        out[part * unit : (part + 1) * unit, side * BLK : (side + 1) * BLK] = ar_full[owner, at : at + unit]
-    gb_ref[:, :BLK] = ar_full[0, per : per + 8].sum(axis=0, keepdims=True)
-    gb_ref[:, BLK:] = ar_full[0, per + 8 : per + 16].sum(axis=0, keepdims=True)
+    full_ref[...] = ar_full[...]
 
     def row_sent(p):
         for r in range(1, row):
@@ -432,15 +461,50 @@
     for k in range(1, col):
         slot_copy(k).wait_send()
         b_copy(k).wait_send()
-        c_copy(k).wait_send()
     for r in range(1, row):
         a_copy(r).wait_send()
         d_copy(r).wait_send()
     for k in range(1, zs):
         own_copy(k).wait_send()
-        w_copy(k).wait_send()
-        sl_copy(k).wait_send()
         agg_copy(z_peer(k)).wait_send()
+    w_rest(True)
+    sl_rest(True)
+
+
+def places(row, fw):
+    per, unit = 4 * fw // row, fw // 2
+    for u in range(8):
+        yield u // 4, (u // 2) % 2, u % 2, u * unit // per, u * unit % per
+
+
+def hand_over_kernel(act, sums, act_out, gn_out, gs_out, gb_out):
+    row, fw = sums.shape[0], gn_out.shape[0]
+    unit, per = fw // 2, 4 * fw // row
+    act_out[...] = act[...]
+    for which, side, part, owner, at in places(row, fw):
+        out = (gn_out, gs_out)[which]
+        piece = sums[owner, at : at + unit].astype(F32)
+        out[part * unit : (part + 1) * unit, side * BLK : (side + 1) * BLK] = piece
+    rows = sums[0, per : per + 16].astype(F32)
+    both = [rows[:8].sum(axis=0, keepdims=True), rows[8:].sum(axis=0, keepdims=True)]
+    gb_out[...] = jnp.concatenate(both, axis=1).reshape(gb_out.shape)
+
+
+def hand_over(activation, sums, fw, width):
+    vmem = pl.BlockSpec(memory_space=pltpu.VMEM)
+    return pl.pallas_call(
+        hand_over_kernel,
+        out_shape=(
+            jax.ShapeDtypeStruct(activation.shape, BF),
+            jax.ShapeDtypeStruct((fw, width), F32),
+            jax.ShapeDtypeStruct((fw, width), F32),
+            jax.ShapeDtypeStruct((width,), F32),
+        ),
+        in_specs=[vmem] * 2,
+        out_specs=(vmem,) * 4,
+        compiler_params=pltpu.CompilerParams(vmem_limit_bytes=56 * 1024 * 1024),
+        name="hand_over",
+    )(activation, sums)
 
 
 def local(row, features, w_neigh, w_self, bias, target_blocks, loc_tiles, loc_src, loc_count, rem_tiles, rem_src,
@@ -454,13 +518,19 @@
     width = w_neigh.shape[1]
     mid = fw // 2
     per = 4 * fw // row
-    chunk = -(-(per + 16) // (8 * col)) * 8 * col
-    hbm = pl.BlockSpec(memory_space=pl.ANY)
+    chunk = per + 16
+    hbm = pl.BlockSpec(memory_space=pltpu.HBM)
     vmem = pl.BlockSpec(memory_space=pltpu.VMEM)
-    smem = pl.BlockSpec(memory_space=pltpu.SMEM)
     dma = pltpu.SemaphoreType.DMA
     scratch = [
-        pltpu.VMEM(features.shape, BF),
+        pltpu.VMEM(bias.shape, F32),
+        pltpu.SMEM(target_blocks.shape, jnp.int32),
+        pltpu.SMEM(loc_src.shape, jnp.int32),
+        pltpu.SMEM(loc_count.shape, jnp.int32),
+        pltpu.SMEM(rem_src.shape, jnp.int32),
+        pltpu.VMEM(rem_slot.shape, jnp.int32),
+        pltpu.VMEM(degree.shape, jnp.int32),
+        pltpu.VMEM(cotangent.shape, BF),
         pltpu.VMEM((nblocks, fw, BLK), BF),
         pltpu.VMEM((col, row, BLK, BLK), BF),
         pltpu.VMEM((targets, slots, BLK, BLK), BF),
@@ -480,44 +550,39 @@
         pltpu.VMEM((zs, mid, BLK), BF),
         pltpu.VMEM((2, zs, fw, width), BF),
         pltpu.VMEM((zs, HALF, width), BF),
-        pltpu.VMEM((row, chunk, BLK), F32),
-        pltpu.VMEM((row, chunk, BLK), F32),
-        pltpu.VMEM((chunk, BLK), F32),
-        pltpu.VMEM((col, chunk // col, BLK), F32),
-        pltpu.VMEM((chunk, BLK), F32),
-        pltpu.VMEM((row, chunk, BLK), F32),
-        dma((4,)), dma((col,)),
+        pltpu.VMEM((row, chunk, BLK), BF),
+        pltpu.VMEM((row, chunk, BLK), BF),
+        pltpu.VMEM((col, chunk, BLK), BF),
+        pltpu.VMEM((row, chunk, BLK), BF),
+        dma((4,)), dma((8,)), dma((nblocks,)), dma((col,)),
         dma((row, col)), dma((row, col)),
         dma((col,)), dma((col,)),
         dma((2, col // 2)), dma((2, col // 2)),
         dma((zs,)), dma((zs,)),
         dma((zs,)), dma((zs,)),
-        dma((zs,)), dma((zs,)),
+        dma((2, zs // 2 + 1)), dma((2, zs // 2 + 1)),
         dma((1,)), dma((1,)),
-        dma((zs,)), dma((zs,)),
+        dma((2, zs // 2 + 1)), dma((2, zs // 2 + 1)),
         dma((row,)), dma((row,)),
-        dma((col,)), dma((col,)),
         dma((col,)), dma((col,)),
         dma((row,)), dma((row,)),
     ]
-    activation, grad_neigh, grad_self, grad_bias = pl.pallas_call(
+    activation, sums = pl.pallas_call(
         functools.partial(kernel, row),
         out_shape=(
             jax.ShapeDtypeStruct(cotangent.shape, BF),
-            jax.ShapeDtypeStruct(w_neigh.shape, F32),
-            jax.ShapeDtypeStruct(w_self.shape, F32),
-            jax.ShapeDtypeStruct((1, width), F32),
+            jax.ShapeDtypeStruct((row, chunk, BLK), BF),
         ),
-        in_specs=[hbm, hbm, hbm, vmem, smem, hbm, smem, smem, hbm, smem, vmem, vmem, vmem],
-        out_specs=(vmem, vmem, vmem, vmem),
+        in_specs=[hbm] * 13,
+        out_specs=(vmem, vmem),
         scratch_shapes=scratch,
         compiler_params=pltpu.CompilerParams(
-            collective_id=0, has_side_effects=True, vmem_limit_bytes=40 * 1024 * 1024
+            collective_id=0, has_side_effects=True, vmem_limit_bytes=56 * 1024 * 1024
         ),
         name="sage_layer",
-    )(features, w_neigh, w_self, bias, target_blocks, loc_tiles, loc_src, loc_count, rem_tiles, rem_src, rem_slot,
+    )(features.T, w_neigh, w_self, bias, target_blocks, loc_tiles, loc_src, loc_count, rem_tiles, rem_src, rem_slot,
       degree, cotangent)
-    return activation, grad_neigh, grad_self, grad_bias.reshape(width)
+    return hand_over(activation, sums, fw, width)
 
 
 def solution(mesh, row=ROW_SIZE):

time: 108 us -> 83.9 us (0.78)
  local copies, waits for them, and re-layouts: 13.6 us -> 0 us
  Pallas kernels: 93.3 us -> 83.1 us
    unnamed x29 -> x0, local copies, waits for them, and re-layouts: 13.6 us -> none
    pallas_call x1, Pallas kernels: 93.3 us -> 81.5 us  [local(): pl.pallas_call(functools.partial(kernel, row), out_shape=(jax.ShapeDtypeS...]
    pallas_call x0 -> x1, Pallas kernels: none -> 1.62 us  [hand_over(): pl.pallas_call(hand_over_kernel, out_shape=(jax.ShapeDtypeStruct(activati...]
where the time goes in v2:
time: 83.9 us; the launch traced here: 83.7 us
  Pallas kernels  83.1 us (99%)
    pallas_call x1, Pallas kernels, local(): pl.pallas_call(functools.partial(kernel, row), out_shape=(jax.ShapeDtypeS...  81.5 us

profile of v2, /device:TPU:1, one launch (start us, length us, event | category | flops | bytes accessed | tf_op | source)
XLA Modules:
  0.0 83.7 jit_solution(1632234327824391070)
XLA Ops:
  0.6 81.5 %sage_layer.1 = (bf16[64,256]{1,0:T(8,128)(2,1)}, bf16[8,64,128]{2,1,0:T(8,128)(2,1)}) custom-call(bf16[96,1024]{1,0:T(8,128)(2,1)} %bitcast.1, bf16[96,256]{1,0:T(8,128)(2,1)} %wn_hbm.1, bf16[96,256]{1,0:T(8,128)(2,1)} %ws_hbm.1, f32[256]{0:T(256)} %bias_hbm.1, s32[6]{0:T(128)} %tb_hbm.1, bf16[6,8,128,128]{3,2,1,0:T(8,128)(2,1)} %loct_hbm.1, ...), custom_call_target="tpu_custom_call" | custom-call | tf_op jit(solution)/shard_map/sage_layer/pallas_call | solution.py:570
  82.1 1.6 %hand_over.1 = (bf16[64,256]{1,0:T(8,128)(2,1)}, f32[96,256]{1,0:T(8,128)}, f32[96,256]{1,0:T(8,128)}, f32[256]{0:T(256)}) custom-call(bf16[64,256]{1,0:T(8,128)(2,1)} %get-tuple-element.6.act, bf16[8,64,128]{2,1,0:T(8,128)(2,1)} %get-tuple-element.7.sums), custom_call_target="tpu_custom_call" | custom-call | tf_op jit(solution)/shard_map/hand_over/pallas_call | solution.py:495

commit v3 on v2

--- a/solution.py
+++ b/solution.py
@@ -13,6 +13,7 @@
 BLK = 128
 HALF = 64
 SLOPE_PHASES = (3, 3)
+FEED = 4
 ROW_SIZE = 8
 
 
@@ -41,7 +42,7 @@
     feat_hbm, wn_hbm, ws_hbm, bias_hbm, tb_hbm, loct_hbm, lsrc_hbm, lcnt_hbm, remt_hbm, rsrc_hbm, rslot_hbm, deg_hbm, cot_hbm,
     act_ref, full_ref,
     bias_ref, tb, lsrc, lcnt, rsrc, rslot, deg_ref, cot_ref,
-    xt, remt, loct, sb, rb, near, pacc, slot_v, slot_m, ring_out, ring_in,
+    xt, remt, loct, sb, rb, near, slot_v, slot_m, ring_out, ring_in,
     own_t, agg_t, own_s, own_r, agg_s, agg_r, wall, sl,
     ar_g, ar_r, ar_y, ar_full,
     ld, ld_small, ld_feat, ld_rem, row_ss, row_rs, slot_ss, slot_rs, ring_ss, ring_rs,
@@ -62,6 +63,8 @@
     fw = xt.shape[1]
     mid = fw // 2
     nblocks = xt.shape[0]
+    groups = ring_rs.shape[2]
+    group = targets // groups
 
     def row_peer(r):
         return y * row + lax.rem(g + r, row)
@@ -99,7 +102,7 @@
             peer = lax.rem(z + sign * (dist - start) + zs, zs)
             part = pl.ds(side * half, half) if 2 * dist == zs else pl.ds(0, rows)
             ref = buffer.at[shard, part]
-            return to_feat(ref, ref, ssem.at[side, dist], rsem.at[side, dist], peer)
+            return to_feat(ref, ref, ssem.at[0], rsem.at[side, dist], peer)
 
         def phase(i):
             low, top = phases[i]
@@ -109,27 +112,21 @@
                 for dist in range(top, low, -1):
                     copy(side, dist, low).start()
 
-        def rest(wait_send):
+        def rest():
             for low, top in phases:
                 for dist in range(low + 1, top + 1):
                     for side in range(2):
-                        if wait_send:
-                            copy(side, dist, low).wait_send()
-                        elif dist < top or dist == zs // 2:
+                        if dist < top or dist == zs // 2:
                             copy(side, dist, low).wait_recv()
 
-        return phase, rest
-
-    barrier = pltpu.get_barrier_semaphore()
-    for r in range(1, row):
-        pl.semaphore_signal(barrier, inc=1, device_id={"nodes": row_peer(r)}, device_id_type=MESH)
-    for k in range(1, col):
-        pl.semaphore_signal(barrier, inc=1, device_id={"nodes": col_peer(k)}, device_id_type=MESH)
-    for k in range(1, zs):
-        pl.semaphore_signal(barrier, inc=1, device_id={"feat": z_peer(k)}, device_id_type=MESH)
+        def sent():
+            every = buffer.at[pl.ds(0, zs - 1)]
+            to_feat(every, every, ssem.at[0], rsem.at[0, 1], z_peer(1)).wait_send()
+
+        return phase, rest, sent
 
     def load_feat(b):
-        return pltpu.make_async_copy(feat_hbm.at[:, pl.ds(b * BLK, BLK)], xt.at[b], ld_feat.at[b])
+        return pltpu.make_async_copy(feat_hbm.at[:, pl.ds(b * BLK, BLK)], xt.at[b], ld_feat.at[0])
 
     small = [
         pltpu.make_async_copy(src, dst, ld_small.at[i])
@@ -148,7 +145,17 @@
     def load_rem(p):
         return pltpu.make_async_copy(remt_hbm.at[0, pl.ds(dest_row(p) * row, row)], remt.at[p], ld_rem.at[p])
 
-    for p in range(col):
+    load_rem(0).start()
+
+    barrier = pltpu.get_barrier_semaphore()
+    for r in range(1, row):
+        pl.semaphore_signal(barrier, inc=1, device_id={"nodes": row_peer(r)}, device_id_type=MESH)
+    for k in range(1, col):
+        pl.semaphore_signal(barrier, inc=1, device_id={"nodes": col_peer(k)}, device_id_type=MESH)
+    for k in range(1, zs):
+        pl.semaphore_signal(barrier, inc=1, device_id={"feat": z_peer(k)}, device_id_type=MESH)
+
+    for p in range(1, col):
         load_rem(p).start()
     for copy in small[1:]:
         copy.start()
@@ -165,9 +172,11 @@
     def _():
         load_ws.start()
 
+    ring_in[0, 0, :, mid:] = jnp.zeros((targets, mid, BLK), BF)
+    ring_in[1, 0, :, :mid] = jnp.zeros((targets, mid, BLK), BF)
+
     small[0].wait()
-    for b in range(nblocks):
-        load_feat(b).wait()
+    pltpu.make_async_copy(xt, xt, ld_feat.at[0]).wait()
 
     def messages(p):
         load_rem(p).wait()
@@ -182,7 +191,7 @@
                 sb[r, p] = message
 
     def row_copy(r, p):
-        return to_node(sb.at[r, p], rb.at[r, p], row_ss.at[r, p], row_rs.at[r, p], row_peer(r))
+        return to_node(sb.at[r, p], rb.at[r, p], row_ss.at[0], row_rs.at[p], row_peer(r))
 
     messages(0)
     slot_v[0] = jnp.zeros(slot_v.shape[1:], jnp.int32)
@@ -191,17 +200,17 @@
     pl.semaphore_wait(barrier, row + col + zs - 3)
 
     def slot_copy(k):
-        return to_node(slot_v.at[0], slot_v.at[k], slot_ss.at[k], slot_rs.at[k], col_peer(k))
+        return to_node(slot_v.at[0], slot_v.at[k], slot_ss.at[0], slot_rs.at[0], col_peer(k))
 
     def own_copy(k):
-        return to_feat(own_s.at[z_peer(k)], own_r.at[z], own_ss.at[k], own_rs.at[k], z_peer(k))
-
-    w_phase, w_rest = relay(wall.at[core], fw, (3, 3), w_ss, w_rs)
-
+        return to_feat(own_s.at[z_peer(k)], own_r.at[z], own_ss.at[0], own_rs.at[0], z_peer(k))
+
+    w_phase, w_rest, w_sent = relay(wall.at[core], fw, (3, 3), w_ss, w_rs)
+
+    for k in range(1, col):
+        slot_copy(k).start()
     for r in range(1, row):
         row_copy(r, 0).start()
-    for k in range(1, col):
-        slot_copy(k).start()
 
     @pl.when(core == 0)
     def _():
@@ -218,7 +227,83 @@
         for r in range(1, row):
             row_copy(r, p).start()
 
-    loop(1, col, more)
+    early = min(FEED, last)
+    loop(1, early, more)
+
+
+    def nearby(t):
+        total = jnp.zeros((fw, BLK), F32)
+        for k in range(lsrc.shape[1]):
+            block = xt[lsrc[t, k]]
+            block = jnp.where(k < lcnt[t], block, jnp.zeros_like(block))
+            total = total + dot_nt(block, loct[t, k])
+        near[t] = total
+
+    def slot_all():
+        rest = slot_v.at[pl.ds(1, col - 1)]
+        return to_node(rest, rest, slot_ss.at[0], slot_rs.at[0], col_peer(1))
+
+    slot_all().wait_recv()
+    slots = pltpu.make_async_copy(slot_v, slot_m, ld.at[3])
+    slots.start()
+    slots.wait()
+
+    def collapse(p, j, start):
+        k = lax.rem(col - delta(p), col)
+        total = start
+        for r in range(row):
+            source = y * row + lax.rem(g - r + row, row)
+            hit = slot_m[k, 0, source] == j
+            message = rb[r, p].astype(F32)
+            total = total + jnp.where(hit, message, jnp.zeros_like(message))
+        return total
+
+    def row_wait(p):
+        others = pl.ds(1, row - 1)
+        to_node(sb.at[others, p], rb.at[others, p], row_ss.at[0], row_rs.at[p], row_peer(1)).wait_recv()
+
+    up = lax.rem(y + 1, col) * row + g
+    down = lax.rem(y + col - 1, col) * row + g
+    sides = (up, down)
+
+    def ring_first(side, q):
+        some, rows = pl.ds(q * group, group), pl.ds(side * mid, mid)
+        return to_node(
+            ring_out.at[0, some, rows],
+            ring_in.at[side, 0, some, rows],
+            ring_ss.at[0],
+            ring_rs.at[side, 0, q],
+            sides[side],
+        )
+
+    def ring_copy(p, q):
+        side, step = (p - 1) % 2, (p - 1) // 2 + 1
+        some = pl.ds(q * group, group)
+        return to_node(
+            ring_out.at[p, some],
+            ring_in.at[side, step, some],
+            ring_ss.at[0],
+            ring_rs.at[side, step, q],
+            sides[side],
+        )
+
+    def ring_wait(side, step, q):
+        if step == 0:
+            ring_first(side, q).wait_recv()
+        else:
+            ring_copy(2 * step - 1 + side, q).wait_recv()
+
+    row_wait(0)
+
+    def start_ring(q):
+        for i in range(group):
+            j = q * group + i
+            ring_out[0, j] = collapse(0, j, jnp.zeros((fw, BLK), F32)).astype(BF)
+        for side in range(2):
+            ring_first(side, q).start()
+
+    loop(0, groups, start_ring)
+    loop(early, col, more)
 
     for copy in small[1:4] + small[5:]:
         copy.wait()
@@ -234,91 +319,24 @@
 
     load_loc.wait()
 
-    def nearby(t):
-        total = jnp.zeros((fw, BLK), F32)
-        for k in range(lsrc.shape[1]):
-            block = xt[lsrc[t, k]]
-            block = jnp.where(k < lcnt[t], block, jnp.zeros_like(block))
-            total = total + dot_nt(block, loct[t, k])
-        near[t] = total
-
-    loop(0, targets, nearby)
-
-
-    for k in range(1, col):
-        slot_copy(k).wait_recv()
-    slots = pltpu.make_async_copy(slot_v, slot_m, ld.at[3])
-    slots.start()
-    slots.wait()
-
-    def collapse(p, j, start):
-        k = lax.rem(col - delta(p), col)
-        total = start
-        for r in range(row):
-            source = y * row + lax.rem(g - r + row, row)
-            hit = slot_m[k, 0, source] == j
-            message = rb[r, p].astype(F32)
-            total = total + jnp.where(hit, message, jnp.zeros_like(message))
-        return total
-
-    def row_wait(p):
-        for r in range(1, row):
-            row_copy(r, p).wait_recv()
-
-    up = lax.rem(y + 1, col) * row + g
-    down = lax.rem(y + col - 1, col) * row + g
-    sides = (up, down)
-
-    def ring_first(side):
-        rows = pl.ds(side * mid, mid)
-        return to_node(
-            ring_out.at[0, :, rows], ring_in.at[side, 0, :, rows], ring_ss.at[side, 0], ring_rs.at[side, 0], sides[side]
-        )
-
-    def ring_copy(p):
-        side, step = (p - 1) % 2, (p - 1) // 2 + 1
-        return to_node(
-            ring_out.at[p], ring_in.at[side, step], ring_ss.at[side, step], ring_rs.at[side, step], sides[side]
-        )
-
-    def ring_wait(side, step):
-        if step == 0:
-            ring_first(side).wait_recv()
-        else:
-            ring_copy(2 * step - 1 + side).wait_recv()
-
-    row_wait(0)
-
-    def start_ring(j):
-        ring_out[0, j] = collapse(0, j, jnp.zeros((fw, BLK), F32)).astype(BF)
-
-    loop(0, targets, start_ring)
-    ring_first(0).start()
-    ring_first(1).start()
-
-    for p in range(1, last):
-        side, step = (p - 1) % 2, (p - 1) // 2
-        row_wait(p)
-
-        def partial(j, p=p):
-            pacc[j] = collapse(p, j, jnp.zeros((fw, BLK), F32))
-
-        loop(0, targets, partial)
-        ring_wait(side, step)
-
-        def merge(j, p=p, side=side, step=step):
-            if step == 0:
-                own = pl.ds(side * mid, mid)
-                other = pl.ds((1 - side) * mid, mid)
-                ring_out[p, j, own] = (pacc[j, own] + ring_in[side, 0, j, own].astype(F32)).astype(BF)
-                ring_out[p, j, other] = pacc[j, other].astype(BF)
-            else:
-                ring_out[p, j] = (pacc[j] + ring_in[side, step, j].astype(F32)).astype(BF)
-
-        loop(0, targets, merge)
-        ring_copy(p).start()
-        if p == 2 and zs > 6:
+    for step in range(reach - 1):
+        for side in range(2):
+            p = 2 * step + 1 + side
+            row_wait(p)
+
+            def pass_on(q, p=p, side=side, step=step):
+                parts = [collapse(p, q * group + i, jnp.zeros((fw, BLK), F32)) for i in range(group)]
+                ring_wait(side, step, q)
+                for i, part in enumerate(parts):
+                    j = q * group + i
+                    ring_out[p, j] = (part + ring_in[side, step, j].astype(F32)).astype(BF)
+                ring_copy(p, q).start()
+
+            loop(0, groups, pass_on)
+        if step == 0 and zs > 6:
             w_phase(1)
+        each = -(-targets // (reach - 1))
+        loop(min(step * each, targets), min((step + 1) * each, targets), nearby)
 
     partner = n + 1 - 2 * core
 
@@ -328,7 +346,7 @@
     def w_take():
         return to_node(wall.at[1 - core], wall.at[1 - core], wc_ss.at[0], wc_rs.at[0], partner)
 
-    w_rest(False)
+    w_rest()
     w_hand().start()
 
     row_wait(last)
@@ -338,8 +356,11 @@
 
     loop(0, targets, finish)
 
-    for k in range(1, zs):
-        own_copy(k).wait_recv()
+    def own_all():
+        rest = pl.ds(0, zs - 1)
+        return to_feat(own_s.at[rest], own_r.at[rest], own_ss.at[0], own_rs.at[0], z_peer(1))
+
+    own_all().wait_recv()
     w_take().wait_recv()
 
     def project(pieces, which):
@@ -351,13 +372,13 @@
 
     self_part = project(own_r, 1) + bias_ref[...].reshape(1, -1)
 
-    ring_wait(0, reach - 1)
-    ring_wait(1, reach - 1)
-
     def agg_copy(dest):
-        return to_feat(agg_s.at[dest], agg_r.at[z], agg_ss.at[dest], agg_rs.at[z], dest)
+        return to_feat(agg_s.at[dest], agg_r.at[z], agg_ss.at[0], agg_rs.at[0], dest)
 
     for j in range(targets):
+        if j % group == 0:
+            ring_wait(0, reach - 1, j // group)
+            ring_wait(1, reach - 1, j // group)
         total = near[j] + ring_in[0, reach - 1, j].astype(F32) + ring_in[1, reach - 1, j].astype(F32)
         degree = deg_ref[pl.ds(j * BLK, BLK)].reshape(1, BLK).astype(F32)
         block = (total / degree).astype(BF)
@@ -375,12 +396,11 @@
             def _(dest=dest, piece=piece):
                 agg_r[dest] = piece
 
-    def agg_wait(k):
-        source = z_peer(k)
-        to_feat(agg_s.at[source], agg_r.at[source], agg_ss.at[source], agg_rs.at[source], source).wait_recv()
-
-    for k in range(1, zs):
-        agg_wait(k)
+    def agg_all():
+        rest = pl.ds(0, zs - 1)
+        return to_feat(agg_s.at[rest], agg_r.at[rest], agg_ss.at[0], agg_rs.at[0], z_peer(1))
+
+    agg_all().wait_recv()
     pre = project(agg_r, 0) + self_part
 
     scale = 0.7978845608028654
@@ -391,12 +411,12 @@
     slope = cdf + pre * (0.5 * (1.0 - inner * inner)) * (scale * (1.0 + 3.0 * cubic * (pre * pre)))
     sl[z] = (cot_ref[...].astype(F32) * slope).astype(BF)
 
-    sl_phase, sl_rest = relay(sl, HALF, SLOPE_PHASES, sl_ss, sl_rs)
+    sl_phase, sl_rest, sl_sent = relay(sl, HALF, SLOPE_PHASES, sl_ss, sl_rs)
     sl_phase(0)
     for i in range(1, len(SLOPE_PHASES)):
         if sum(SLOPE_PHASES[:i]) < zs // 2:
             sl_phase(i)
-    sl_rest(False)
+    sl_rest()
 
     width = sl.shape[-1]
     grad_n = jnp.zeros((fw, width), F32)
@@ -416,59 +436,54 @@
     for owner in range(row):
         ar_g[owner, per : per + 16] = bias_part
 
+    others = pl.ds(1, row - 1)
+
     def a_copy(r):
-        return to_node(ar_g.at[lax.rem(g + r, row)], ar_r.at[r], a_ss.at[r], a_rs.at[r], row_peer(r))
+        return to_node(ar_g.at[lax.rem(g + r, row)], ar_r.at[r], a_ss.at[0], a_rs.at[0], row_peer(r))
 
     for r in range(1, row):
         a_copy(r).start()
     total = ar_g[g].astype(F32)
+    a_all = to_node(ar_g.at[others], ar_r.at[others], a_ss.at[0], a_rs.at[0], row_peer(1))
+    a_all.wait_recv()
     for r in range(1, row):
-        a_copy(r).wait_recv()
         total = total + ar_r[r].astype(F32)
     ar_y[y] = total.astype(BF)
 
     def b_copy(k):
-        return to_node(ar_y.at[y], ar_y.at[y], b_ss.at[k], b_rs.at[k], col_peer(k))
+        return to_node(ar_y.at[y], ar_y.at[y], b_ss.at[0], b_rs.at[0], col_peer(k))
 
     for k in range(1, col):
         b_copy(k).start()
-    for k in range(1, col):
-        b_copy(k).wait_recv()
+    b_rest = ar_y.at[pl.ds(0, col - 1)]
+    b_all = to_node(b_rest, b_rest, b_ss.at[0], b_rs.at[0], col_peer(1))
+    b_all.wait_recv()
     total = ar_y[0].astype(F32)
     for k in range(1, col):
         total = total + ar_y[k].astype(F32)
     ar_full[g] = total.astype(BF)
 
     def d_copy(r):
-        return to_node(ar_full.at[g], ar_full.at[g], d_ss.at[r], d_rs.at[r], row_peer(r))
+        return to_node(ar_full.at[g], ar_full.at[g], d_ss.at[0], d_rs.at[0], row_peer(r))
 
     for r in range(1, row):
         d_copy(r).start()
-    for r in range(1, row):
-        d_copy(r).wait_recv()
+    d_rest = ar_full.at[pl.ds(0, row - 1)]
+    d_all = to_node(d_rest, d_rest, d_ss.at[0], d_rs.at[0], row_peer(1))
+    d_all.wait_recv()
     full_ref[...] = ar_full[...]
 
-    def row_sent(p):
-        for r in range(1, row):
-            row_copy(r, p).wait_send()
-
-    loop(0, col, row_sent)
-    for side in range(2):
-        ring_first(side).wait_send()
-    for p in range(1, last):
-        ring_copy(p).wait_send()
+    to_node(sb.at[others], rb.at[others], row_ss.at[0], row_rs.at[0], row_peer(1)).wait_send()
+    to_node(ring_out, ring_out, ring_ss.at[0], ring_rs.at[0, 0, 0], up).wait_send()
     w_hand().wait_send()
-    for k in range(1, col):
-        slot_copy(k).wait_send()
-        b_copy(k).wait_send()
-    for r in range(1, row):
-        a_copy(r).wait_send()
-        d_copy(r).wait_send()
-    for k in range(1, zs):
-        own_copy(k).wait_send()
-        agg_copy(z_peer(k)).wait_send()
-    w_rest(True)
-    sl_rest(True)
+    slot_all().wait_send()
+    own_all().wait_send()
+    agg_all().wait_send()
+    a_all.wait_send()
+    b_all.wait_send()
+    d_all.wait_send()
+    w_sent()
+    sl_sent()
 
 
 def places(row, fw):
@@ -519,6 +534,7 @@
     mid = fw // 2
     per = 4 * fw // row
     chunk = per + 16
+    groups = 2 if targets % 2 == 0 else 1
     hbm = pl.BlockSpec(memory_space=pltpu.HBM)
     vmem = pl.BlockSpec(memory_space=pltpu.VMEM)
     dma = pltpu.SemaphoreType.DMA
@@ -537,7 +553,6 @@
         pltpu.VMEM((row, col, fw, BLK), BF),
         pltpu.VMEM((row, col, fw, BLK), BF),
         pltpu.VMEM((targets, fw, BLK), F32),
-        pltpu.VMEM((targets, fw, BLK), F32),
         pltpu.VMEM((col, 8, BLK), jnp.int32),
         pltpu.SMEM((col, 8, BLK), jnp.int32),
         pltpu.VMEM((col - 1, targets, fw, BLK), BF),
@@ -554,18 +569,18 @@
         pltpu.VMEM((row, chunk, BLK), BF),
         pltpu.VMEM((col, chunk, BLK), BF),
         pltpu.VMEM((row, chunk, BLK), BF),
-        dma((4,)), dma((8,)), dma((nblocks,)), dma((col,)),
-        dma((row, col)), dma((row, col)),
-        dma((col,)), dma((col,)),
-        dma((2, col // 2)), dma((2, col // 2)),
-        dma((zs,)), dma((zs,)),
-        dma((zs,)), dma((zs,)),
-        dma((2, zs // 2 + 1)), dma((2, zs // 2 + 1)),
+        dma((4,)), dma((8,)), dma((1,)), dma((col,)),
+        dma((1,)), dma((col,)),
         dma((1,)), dma((1,)),
-        dma((2, zs // 2 + 1)), dma((2, zs // 2 + 1)),
-        dma((row,)), dma((row,)),
-        dma((col,)), dma((col,)),
-        dma((row,)), dma((row,)),
+        dma((1,)), dma((2, col // 2, groups)),
+        dma((1,)), dma((1,)),
+        dma((1,)), dma((1,)),
+        dma((1,)), dma((2, zs // 2 + 1)),
+        dma((1,)), dma((1,)),
+        dma((1,)), dma((2, zs // 2 + 1)),
+        dma((1,)), dma((1,)),
+        dma((1,)), dma((1,)),
+        dma((1,)), dma((1,)),
     ]
     activation, sums = pl.pallas_call(
         functools.partial(kernel, row),

time: 83.9 us -> 80.7 us (0.962)
  Pallas kernels: 83.1 us -> 79.9 us
    pallas_call x1, Pallas kernels: 81.5 us -> 78.3 us  [local(): pl.pallas_call(functools.partial(kernel, row), out_shape=(jax.ShapeDtypeS...]
where the time goes in v3:
time: 80.7 us; the launch traced here: 80.5 us
  Pallas kernels  79.9 us (99%)
    pallas_call x1, Pallas kernels, local(): pl.pallas_call(functools.partial(kernel, row), out_shape=(jax.ShapeDtypeS...  78.3 us
    pallas_call x1, Pallas kernels, hand_over(): pl.pallas_call(hand_over_kernel, out_shape=(jax.ShapeDtypeStruct(activati...  1.62 us

profile of v3, /device:TPU:1, one launch (start us, length us, event | category | flops | bytes accessed | tf_op | source)
XLA Modules:
  0.0 80.5 jit_solution(9817898614146701893)
XLA Ops:
  0.6 78.3 %sage_layer.1 = (bf16[64,256]{1,0:T(8,128)(2,1)}, bf16[8,64,128]{2,1,0:T(8,128)(2,1)}) custom-call(bf16[96,1024]{1,0:T(8,128)(2,1)} %bitcast.1, bf16[96,256]{1,0:T(8,128)(2,1)} %wn_hbm.1, bf16[96,256]{1,0:T(8,128)(2,1)} %ws_hbm.1, f32[256]{0:T(256)} %bias_hbm.1, s32[6]{0:T(128)} %tb_hbm.1, bf16[6,8,128,128]{3,2,1,0:T(8,128)(2,1)} %loct_hbm.1, ...), custom_call_target="tpu_custom_call" | custom-call | tf_op jit(solution)/shard_map/sage_layer/pallas_call | solution.py:585
  78.9 1.6 %hand_over.1 = (bf16[64,256]{1,0:T(8,128)(2,1)}, f32[96,256]{1,0:T(8,128)}, f32[96,256]{1,0:T(8,128)}, f32[256]{0:T(256)}) custom-call(bf16[64,256]{1,0:T(8,128)(2,1)} %get-tuple-element.6.act, bf16[8,64,128]{2,1,0:T(8,128)(2,1)} %get-tuple-element.7.sums), custom_call_target="tpu_custom_call" | custom-call | tf_op jit(solution)/shard_map/hand_over/pallas_call | solution.py:510

commit v4 on v3

--- a/solution.py
+++ b/solution.py
@@ -439,13 +439,14 @@
     others = pl.ds(1, row - 1)
 
     def a_copy(r):
-        return to_node(ar_g.at[lax.rem(g + r, row)], ar_r.at[r], a_ss.at[0], a_rs.at[0], row_peer(r))
+        return to_node(ar_g.at[lax.rem(g + r, row)], ar_r.at[g], a_ss.at[0], a_rs.at[0], row_peer(r))
 
     for r in range(1, row):
         a_copy(r).start()
-    total = ar_g[g].astype(F32)
+    ar_r[g] = ar_g[g]
     a_all = to_node(ar_g.at[others], ar_r.at[others], a_ss.at[0], a_rs.at[0], row_peer(1))
     a_all.wait_recv()
+    total = ar_r[0].astype(F32)
     for r in range(1, row):
         total = total + ar_r[r].astype(F32)
     ar_y[y] = total.astype(BF)
@@ -461,17 +462,20 @@
     total = ar_y[0].astype(F32)
     for k in range(1, col):
         total = total + ar_y[k].astype(F32)
-    ar_full[g] = total.astype(BF)
+    ar_full[g, :per] = total[:per].astype(BF)
+
+    for r in range(row):
+        full_ref[r, per:] = total[per:].astype(BF)
 
     def d_copy(r):
-        return to_node(ar_full.at[g], ar_full.at[g], d_ss.at[0], d_rs.at[0], row_peer(r))
+        return to_node(ar_full.at[g, pl.ds(0, per)], ar_full.at[g, pl.ds(0, per)], d_ss.at[0], d_rs.at[0], row_peer(r))
 
     for r in range(1, row):
         d_copy(r).start()
-    d_rest = ar_full.at[pl.ds(0, row - 1)]
+    d_rest = ar_full.at[pl.ds(0, row - 1), pl.ds(0, per)]
     d_all = to_node(d_rest, d_rest, d_ss.at[0], d_rs.at[0], row_peer(1))
     d_all.wait_recv()
-    full_ref[...] = ar_full[...]
+    full_ref[:, :per] = ar_full[:, :per]
 
     to_node(sb.at[others], rb.at[others], row_ss.at[0], row_rs.at[0], row_peer(1)).wait_send()
     to_node(ring_out, ring_out, ring_ss.at[0], ring_rs.at[0, 0, 0], up).wait_send()

time: 80.7 us -> 80.7 us (level)
  no operation moved by 1% of the time
where the time goes in v4:
time: 80.7 us; the launch traced here: 80.4 us
  Pallas kernels  79.7 us (99%)
    pallas_call x1, Pallas kernels, local(): pl.pallas_call(functools.partial(kernel, row), out_shape=(jax.ShapeDtypeS...  78.1 us
    pallas_call x1, Pallas kernels, hand_over(): pl.pallas_call(hand_over_kernel, out_shape=(jax.ShapeDtypeStruct(activati...  1.62 us

profile of v4, /device:TPU:1, one launch (start us, length us, event | category | flops | bytes accessed | tf_op | source)
XLA Modules:
  0.0 80.4 jit_solution(2610462049628655945)
XLA Ops:
  0.6 78.1 %sage_layer.1 = (bf16[64,256]{1,0:T(8,128)(2,1)}, bf16[8,64,128]{2,1,0:T(8,128)(2,1)}) custom-call(bf16[96,1024]{1,0:T(8,128)(2,1)} %bitcast.1, bf16[96,256]{1,0:T(8,128)(2,1)} %wn_hbm.1, bf16[96,256]{1,0:T(8,128)(2,1)} %ws_hbm.1, f32[256]{0:T(256)} %bias_hbm.1, s32[6]{0:T(128)} %tb_hbm.1, bf16[6,8,128,128]{3,2,1,0:T(8,128)(2,1)} %loct_hbm.1, ...), custom_call_target="tpu_custom_call" | custom-call | tf_op jit(solution)/shard_map/sage_layer/pallas_call | solution.py:589
  78.8 1.6 %hand_over.1 = (bf16[64,256]{1,0:T(8,128)(2,1)}, f32[96,256]{1,0:T(8,128)}, f32[96,256]{1,0:T(8,128)}, f32[256]{0:T(256)}) custom-call(bf16[64,256]{1,0:T(8,128)(2,1)} %get-tuple-element.6.act, bf16[8,64,128]{2,1,0:T(8,128)(2,1)} %get-tuple-element.7.sums), custom_call_target="tpu_custom_call" | custom-call | tf_op jit(solution)/shard_map/hand_over/pallas_call | solution.py:514
